TPU v7x, 512 devices: a whole 4x8x8 slice. The times are simulated.
512 devices in a mesh: wide: 128 (over y, z, core), narrow: 4 (over x).
Axes of the slice: x: 4, y: 8, z: 8, core: 2. Of those that a mesh axis runs over, the one named last changes fastest.
Arguments:
- iv_curves: bfloat16 [32768, 8192], P('wide', 'narrow'), may hold values from -25 to 25
- mean_curve: float32 [8192], P('narrow'), may hold values from -4 to 4
- loadings: bfloat16 [8192, 256], P('narrow'), may hold values from -0.0625 to 0.0625
- metrology: bfloat16 [32768, 2048], P('wide', 'narrow'), may hold values from -35 to 35
- dest_owner: int32 [32768], P('wide'), may hold values from 0 to 127, as said below
- dest_row: int32 [32768], P('wide'), may hold values from 0 to 255, as said below
Outputs:
- residual_msq: float32 [32768], P(('wide', 'narrow'))
- cross_z: float32 [256, 2048], P('wide', 'narrow')
Inputs may be any that keep to these rules, and one draw needn't show every extreme that they name: Together with dest_row it names each wafer-order row dest_owner * 256 + dest_row exactly once, so every wide index owns the rows of 256 dies. The number of dies that wide index s sends to wide index o depends only on (o - s) modulo the wide axis's length; it is at most 4 and equals 4 for some offset. `dest_row`: see dest_owner.
All inputs are finite; a program needn't handle non-finite values.
Results may differ from a plain program's by a relative error of at most 0.0056.
Values may be sent and summed in bfloat16 or wider, within the bound.
A program may use at most 64 MiB of HBM per device.

v0:
```python
import math

import jax
import jax.numpy as jnp
from jax import lax
from jax.sharding import PartitionSpec as P

EPSILON = 1e-05


def pack_rows(values, flat_slot, wide_count, slot_count):
    holder = jnp.zeros((wide_count * slot_count, values.shape[1]), values.dtype)
    return holder.at[flat_slot].set(values).reshape(wide_count, slot_count, values.shape[1])


def standardize(values, total, square, die_total):
    center = total / die_total
    scaling = lax.rsqrt(square / die_total - center * center + EPSILON)
    return ((values - center) * scaling).astype(jnp.bfloat16)


def shards(iv_curves, mean_curve, loadings, metrology, dest_owner, dest_row):
    wide_count = lax.axis_size("wide")
    narrow_count = lax.axis_size("narrow")
    die_count = iv_curves.shape[0]
    total_dies = die_count * wide_count
    feature_count = loadings.shape[0] * narrow_count
    comp_count = loadings.shape[1]
    slot_count = 2 * die_count // wide_count
    owners = jnp.arange(wide_count, dtype=jnp.int32)
    member = (dest_owner[:, None] == owners[None, :]).astype(jnp.int32)
    earlier = jnp.cumsum(member, axis=0) - member
    flat_slot = dest_owner * slot_count + jnp.sum(earlier * member, axis=1)
    slot_rows = (
        jnp.full((wide_count * slot_count,), die_count, jnp.int32).at[flat_slot].set(dest_row)
    )
    slot_rows = slot_rows.reshape(wide_count, slot_count)
    centered = (iv_curves.astype(jnp.float32) - mean_curve[None, :]).astype(jnp.bfloat16)
    partial_value = jnp.dot(centered, loadings, preferred_element_type=jnp.float32)
    metro_f = metrology.astype(jnp.float32)
    metro_total = jnp.sum(metro_f, axis=0)
    metro_square = jnp.sum(metro_f * metro_f, axis=0)
    scores = lax.psum(partial_value, "narrow")
    sums = lax.psum(
        (jnp.sum(scores, axis=0), jnp.sum(scores * scores, axis=0), metro_total, metro_square),
        "wide",
    )
    score_z = standardize(scores, sums[0], sums[1], total_dies)
    metro_z = standardize(metro_f, sums[2], sums[3], total_dies)
    score_bf = scores.astype(jnp.bfloat16)
    arrived, arrived_rows = (
        lax.all_to_all(
            pack_rows(score_z, flat_slot, wide_count, slot_count),
            "wide",
            split_axis=0,
            concat_axis=0,
            tiled=True,
        ),
        lax.all_to_all(slot_rows, "wide", split_axis=0, concat_axis=0, tiled=True),
    )
    placed = jnp.zeros((die_count, comp_count), jnp.bfloat16)
    placed = placed.at[arrived_rows.reshape(-1)].set(arrived.reshape(-1, comp_count), mode="drop")
    rebuilt = lax.dot_general(
        score_bf, loadings, (((1,), (1,)), ((), ())), preferred_element_type=jnp.float32
    )
    residue = centered.astype(jnp.float32) - rebuilt
    residual_msq = lax.psum_scatter(
        jnp.sum(residue * residue, axis=1) / feature_count,
        "narrow",
        scatter_dimension=0,
        tiled=True,
    )
    scaling = 1.0 / math.sqrt(total_dies)
    cross_z = lax.psum_scatter(
        lax.dot_general(
            placed, metro_z, (((0,), (0,)), ((), ())), preferred_element_type=jnp.float32
        )
        * scaling,
        "wide",
        scatter_dimension=0,
        tiled=True,
    )
    return (residual_msq, cross_z)


def solution(mesh):
    in_specs = (
        P("wide", "narrow"),
        P("narrow"),
        P("narrow", None),
        P("wide", "narrow"),
        P("wide"),
        P("wide"),
    )
    out_specs = (P(("wide", "narrow")), P("wide", "narrow"))
    return jax.shard_map(shards, mesh=mesh, in_specs=in_specs, out_specs=out_specs, check_vma=False)
```

profile of v0, /device:TPU:24, one launch (start us, length us, event | category | flops | bytes accessed | tf_op | source)
XLA Modules:
  0.0 543.7 jit_solution(7650720094755950593)
XLA Ops:
  7.2 0.0 all-reduce.6.cloned.1.call-start
  7.2 1.2 copy-done
  8.4 2.4 fusion.2
  10.8 0.0 all-reduce.6.cloned.1.call-update
  10.8 0.1 copy.10
  10.9 0.2 fusion.9
  11.2 0.2 fusion.12
  11.4 1.6 scatter_custom_fusion
  13.0 0.7 all_to_all.9
  13.7 17.3 %all-to-all-start = ((s32[128,1,4]{2,1,0:T(1,128)}), s32[128,1,4]{2,1,0:T(1,128)S(1)}, u32[]{:S(2)}, u32[]{:S(2)}) async-start(s32[128,1,4]{2,1,0:T(1,128)} %bitcast.4), calls=%async_computation | async-start | bytes 131072 | tf_op jit(solution)/shard_map/all_to_all | solution.py:59
  31.1 0.1 convert_reduce_fusion
  31.1 36.6 %all-reduce.6.cloned.1.call-done = f32[256,256]{1,0:T(8,128)} async-done(((f32[256,256]{1,0:T(8,128)}), f32[256,256]{1,0:T(8,128)}) %all-reduce.6.cloned.1.call-update) | async-done | bytes 262160 | tf_op jit(solution)/shard_map/psum | solution.py:43
  67.7 1.0 fusion.23
  68.7 217.4 %all-reduce.2 = (f32[256]{0:T(256)S(1)}, f32[256]{0:T(256)S(1)}, f32[512]{0:T(512)S(1)}, f32[512]{0:T(512)S(1)}) all-reduce(f32[256]{0:T(256)S(1)} %get-tuple-element.5, f32[256]{0:T(256)S(1)} %get-tuple-element.4, f32[512]{0:T(512)S(1)} %get-tuple-element.3, ...), channel_id=1, replica_groups=mesh['wide'=128,'narrow'=4] {'wide'}, use_global_device_ids=true, to_apply=%region_10.11 | all-reduce | flops 1536 | bytes 12288 | tf_op jit(solution)/shard_map/psum | solution.py:44
  286.1 2.0 scatter_custom_fusion.1
  288.1 0.8 reshape.69
  288.9 43.5 %all-to-all-start.1 = ((bf16[128,4,256]{2,1,0:T(4,128)(2,1)}), bf16[128,4,256]{2,1,0:T(4,128)(2,1)S(1)}, u32[]{:S(2)}, u32[]{:S(2)}) async-start(bf16[128,4,256]{2,1,0:T(4,128)(2,1)} %reshape.69), calls=%async_computation.1 | async-start | bytes 524288 | tf_op jit(solution)/shard_map/all_to_all | solution.py:52
  332.4 0.0 all-reduce.8.cloned.1.call-start
  332.4 1.3 dynamic-slice.2
  333.7 1.3 dynamic-slice
  336.2 0.5 broadcast.82
  336.8 0.8 reduce.3
  337.6 0.1 reshape.68
  337.7 7.7 %all-to-all-done.1 = bf16[128,4,256]{2,1,0:T(4,128)(2,1)S(1)} async-done(((bf16[128,4,256]{2,1,0:T(4,128)(2,1)}), bf16[128,4,256]{2,1,0:T(4,128)(2,1)S(1)}, u32[]{:S(2)}, u32[]{:S(2)}) %all-to-all-start.1) | async-done | bytes 262176 | tf_op jit(solution)/shard_map/all_to_all | solution.py:52
  345.4 0.1 reshape.91
  345.5 2.3 scatter_custom_fusion.2
  347.8 1.1 convolution_multiply_fusion
  349.0 0.6 fusion.1
  349.6 9.6 %all-reduce = f32[256]{0:T(256)S(1)} all-reduce(f32[256]{0:T(256)S(1)} %broadcast_multiply_fusion.2), channel_id=2, replica_groups=mesh['wide'=128,'narrow'=4] {'narrow'}, use_global_device_ids=true, to_apply=%region_2.3.clone | all-reduce | flops 256 | bytes 2048
  359.2 0.6 dynamic-slice.1
  359.8 175.7 %all-reduce.8.cloned.1.call-done = f32[256,512]{1,0:T(8,128)} async-done(((f32[256,512]{1,0:T(8,128)}), f32[256,512]{1,0:T(8,128)}) %all-reduce.8.cloned.1.call-update) | async-done | bytes 524304
  535.5 1.3 constant_dynamic-slice_fusion
  (24 shorter events, 0.2 us)
Async XLA Ops:
  7.2 1.2 copy-start
  7.2 3.6 copy-start.3
  7.2 60.5 %all-reduce.6.cloned.1.call-start = ((), (), s32[]{:S(2)}) async-start(), calls=%async_computation.2 | async-start | bytes 524288 | tf_op jit(solution)/shard_map/psum | solution.py:43
  10.8 20.3 %copy-start.1 = (bf16[256,512]{1,0:T(8,128)(2,1)S(1)}, bf16[256,512]{1,0:T(8,128)(2,1)}, u32[]{:S(2)}) copy-start(bf16[256,512]{1,0:T(8,128)(2,1)} %param.9) | copy-start | bytes 786436
  13.7 275.2 %all-to-all-start = ((s32[128,1,4]{2,1,0:T(1,128)}), s32[128,1,4]{2,1,0:T(1,128)S(1)}, u32[]{:S(2)}, u32[]{:S(2)}) async-start(s32[128,1,4]{2,1,0:T(1,128)} %bitcast.4), calls=%async_computation | async-start | bytes 131072 | tf_op jit(solution)/shard_map/all_to_all | solution.py:59
  288.9 56.6 %all-to-all-start.1 = ((bf16[128,4,256]{2,1,0:T(4,128)(2,1)}), bf16[128,4,256]{2,1,0:T(4,128)(2,1)S(1)}, u32[]{:S(2)}, u32[]{:S(2)}) async-start(bf16[128,4,256]{2,1,0:T(4,128)(2,1)} %reshape.69), calls=%async_computation.1 | async-start | bytes 524288 | tf_op jit(solution)/shard_map/all_to_all | solution.py:52
  332.4 203.2 %all-reduce.8.cloned.1.call-start = ((), (), s32[]{:S(2)}) async-start(), calls=%async_computation.3 | async-start | bytes 1048576
  337.7 11.2 %copy-start.2 = (f32[256,256]{1,0:T(8,128)S(1)}, f32[256,256]{1,0:T(8,128)}, u32[]{:S(2)}) copy-start(f32[256,256]{1,0:T(8,128)} %all-reduce.6.cloned.1.call-done) | copy-start | bytes 786436
  337.7 11.2 %copy-start.4 = (bf16[256,2048]{1,0:T(8,128)(2,1)S(1)}, bf16[256,2048]{1,0:T(8,128)(2,1)}, u32[]{:S(2)}) copy-start(bf16[256,2048]{1,0:T(8,128)(2,1)} %param.6) | copy-start | bytes 3145732
  337.7 11.2 %copy-start.5 = (f32[2048]{0:T(1024)S(1)}, f32[2048]{0:T(1024)}, u32[]{:S(2)}) copy-start(f32[2048]{0:T(1024)} %param.7) | copy-start | bytes 24580
Sparse Core Ops, SparseCore 0:
  10.9 56.7 all-reduce.5
  349.1 186.4 all-reduce.7
where the time goes:
time: 544 us
  blocking collectives  227 us (42%)
  waiting for transfers between devices  220 us (40%)
  starting transfers between devices  60.9 us (11%)
  between operations  15.5 us (3%)
  local copies, waits for them, and re-layouts  11.8 us (2%)
    psum x1, blocking collectives, shards(): lax.psum((jnp.sum(scores, axis=0), jnp.sum(scores * scores, axis=0), metr...  217 us
    unnamed x3, waiting for transfers between devices  176 us
    all_to_all x1, starting transfers between devices, shards(): lax.all_to_all(pack_rows(score_z, flat_slot, wide_count, slot_count), 'wi...  43.5 us
    psum x1, waiting for transfers between devices, shards(): scores = lax.psum(partial_value, 'narrow')  36.6 us
    all_to_all x1, starting transfers between devices, shards(): lax.all_to_all(slot_rows, 'wide', split_axis=0, concat_axis=0, tiled=True)  17.3 us
  transfers between devices with their start and end apart: 4, of which 3 were waited for; matrix products, arithmetic and copies ran while one was open for 2% of the time, Pallas kernels for 0%

commit v1 on v0

v1 whole, which is shorter than its diff:
```python
import functools
import math

import jax
import jax.numpy as jnp
from jax import lax
from jax.experimental import pallas as pl
from jax.experimental.pallas import tpu as pltpu
from jax.sharding import PartitionSpec as P

EPSILON = 1e-05
MESH = pl.DeviceIdType.MESH
F32 = jnp.float32
BF16 = jnp.bfloat16

NY, NZ, NC, NX = 8, 8, 2, 4
CHIPS = NY * NZ
GROUP = NC * NX
DIES_DEV = 256
FEAT = 2048
COMP = 256
SLICE = COMP // GROUP
METRO = 512
TOTAL = DIES_DEV * CHIPS * NC
CHUNKS = 4
FAR = (4, 3, 5, 2, 6, 1, 7)
(S_ROUTE, S_SCORE, S_MET_X, S_MET_C, S_M1, S_M2, S_M3, S_R1, S_R2, S_CHIP, S_BACK, S_RES, S_OUT) = range(13)
N_SEM = 13


def body(
    iv_hbm, mean_hbm, load_hbm, met_hbm, own_hbm, row_hbm,
    res_out, cross_out,
    iv_v, mean_v, load_v, cen_v, pt_v, met_v, mz_v, route_v,
    asnd, arcv, st_v, bsnd, brcv, oh_v, ohr_v,
    csnd, crcv, dsnd, drcv,
    m1snd, m1rcv, m2snd, m2rcv, m3snd, m3rcv,
    r1snd, r1rcv, r2snd, r2rcv, esnd, ercv,
    ld_sem, ssem, rsem, plane_sem,
):
    w = lax.axis_index("wide")
    n = lax.axis_index("narrow")
    y, z, c = w // 16, (w // 2) % 8, w % 2
    me8 = c * NX + n
    chip = y * NZ + z

    def dev(yy, zz, cc, nn):
        return (yy * 16 + zz * 2 + cc, nn)

    def send(k, src, dst, device):
        pltpu.make_async_remote_copy(
            src_ref=src, dst_ref=dst, send_sem=ssem.at[k], recv_sem=rsem.at[k],
            device_id=device, device_id_type=MESH,
        ).start()

    def got(k, ref):
        pltpu.make_async_copy(ref, ref, rsem.at[k]).wait()

    def sent(k, ref):
        pltpu.make_async_copy(ref, ref, ssem.at[k]).wait()

    group_peers = [((c + dc) % NC, (n + dn) % NX) for dn in (2, 1, 3, 0) for dc in (0, 1) if (dc, dn) != (0, 0)]
    z_peers = [(z + d) % NZ for d in FAR]
    y_peers = [(y + d) % NY for d in FAR]

    step = FEAT // CHUNKS
    loads = []
    for j in range(CHUNKS):
        span = pl.ds(j * step, step)
        loads.append((
            pltpu.make_async_copy(iv_hbm.at[:, span], iv_v.at[:, span], ld_sem.at[2 * j]),
            pltpu.make_async_copy(load_hbm.at[span], load_v.at[span], ld_sem.at[2 * j + 1]),
        ))
    mean_load = pltpu.make_async_copy(mean_hbm, mean_v, ld_sem.at[2 * CHUNKS])
    met_load = pltpu.make_async_copy(met_hbm, met_v.at[me8], ld_sem.at[2 * CHUNKS + 1])
    own_load = pltpu.make_async_copy(own_hbm, route_v.at[c, 0], ld_sem.at[2 * CHUNKS + 2])
    row_load = pltpu.make_async_copy(row_hbm, route_v.at[c, 1], ld_sem.at[2 * CHUNKS + 3])
    mean_load.start()
    for a, b in loads:
        a.start()
        b.start()
    met_load.start()
    own_load.start()
    row_load.start()

    barrier = pltpu.get_barrier_semaphore()
    for zz in z_peers:
        pl.semaphore_signal(barrier, inc=1, device_id=dev(y, zz, c, n), device_id_type=MESH)
    for yy in y_peers:
        pl.semaphore_signal(barrier, inc=1, device_id=dev(yy, z, c, n), device_id_type=MESH)
    for cc, nn in group_peers:
        pl.semaphore_signal(barrier, inc=1, device_id=dev(y, z, cc, nn), device_id_type=MESH)

    mean_load.wait()
    part = jnp.zeros((DIES_DEV, COMP), F32)
    for j, (a, b) in enumerate(loads):
        a.wait()
        b.wait()
        span = pl.ds(j * step, step)
        cen = (iv_v[:, span].astype(F32) - mean_v[:, span]).astype(BF16)
        cen_v[:, span] = cen
        part = part + jnp.dot(cen, load_v[span, :], preferred_element_type=F32)
    pt_v[...] = part.T
    for q in range(GROUP):
        for yy in range(NY):
            asnd[q, 4 * yy:4 * yy + 4, :] = pt_v[pl.ds(32 * yy + 4 * ((q + yy) % NZ), 4), :]

    met_load.wait()
    met = met_v[me8].astype(F32)
    tot = jnp.sum(met, axis=0, keepdims=True)
    sq = jnp.sum(met * met, axis=0, keepdims=True)
    for t in range(4):
        m1snd[t:t + 1, :] = tot[:, 128 * t:128 * t + 128]
        m1snd[4 + t:5 + t, :] = sq[:, 128 * t:128 * t + 128]
    own_load.wait()
    row_load.wait()

    pl.semaphore_wait(barrier, len(z_peers) + len(y_peers) + len(group_peers))

    for cc, nn in group_peers:
        q = cc * NX + nn
        send(S_SCORE, asnd.at[q], arcv.at[me8], dev(y, z, cc, nn))
    send(S_ROUTE, route_v.at[c], route_v.at[c], dev(y, z, 1 - c, n))
    for zz in z_peers:
        send(S_M1, m1snd, m1rcv.at[z], dev(y, zz, c, n))
    for yy in y_peers:
        pl.semaphore_signal(plane_sem, inc=1, device_id=dev(yy, z, c, n), device_id_type=MESH)
    for dn in (2, 1, 3):
        send(S_MET_X, met_v.at[me8], met_v.at[me8], dev(y, z, c, (n + dn) % NX))
    send(S_MET_C, met_v.at[me8], met_v.at[me8], dev(y, z, 1 - c, n))
    arcv[me8] = asnd[me8]
    m1rcv[z] = m1snd[...]

    got(S_ROUTE, route_v.at[0])
    targets, lanes, zds, rows1 = [], [], [], []
    for cs in range(NC):
        owner = jnp.concatenate([route_v[cs, 0, 0:1, :], route_v[cs, 0, 1:2, :]], axis=1)
        row = jnp.concatenate([route_v[cs, 1, 0:1, :], route_v[cs, 1, 1:2, :]], axis=1)
        wide_o = jnp.broadcast_to(owner.astype(F32), (DIES_DEV, DIES_DEV))
        before = lax.broadcasted_iota(jnp.int32, (DIES_DEV, DIES_DEV), 0) < lax.broadcasted_iota(
            jnp.int32, (DIES_DEV, DIES_DEV), 1)
        same = jnp.where((wide_o.T == wide_o) & before, 1.0, 0.0)
        rank = jnp.sum(same, axis=0, keepdims=True).astype(jnp.int32)
        oc = owner & 1
        och = owner >> 1
        r = 2 * oc + cs
        targets.append(rank * 256 + r * 64 + och)
        lanes.append((och >> 3) * 16 + r * 4 + rank)
        zds.append(och & 7)
        rows1.append((row + 1).astype(F32))
    target = jnp.concatenate(targets, axis=1)
    lane = jnp.concatenate(lanes, axis=1)
    zd = jnp.concatenate(zds, axis=1)
    row1 = jnp.concatenate(rows1, axis=1)
    two = NC * DIES_DEV
    left = jnp.where(lax.broadcasted_iota(jnp.int32, (8, two), 0) == zd, row1, 0.0).astype(BF16)
    right = jnp.where(lax.broadcasted_iota(jnp.int32, (128, two), 0) == lane, 1.0, 0.0).astype(BF16)
    table = lax.dot_general(left, right, (((1,), (1,)), ((), ())), preferred_element_type=F32)
    for zz in range(NZ):
        r1snd[zz] = table[zz:zz + 1, :]
    for zz in z_peers:
        send(S_R1, r1snd.at[zz], r1rcv.at[z], dev(y, zz, c, n))
    r1rcv[z] = r1snd[z]
    for l in range(4):
        oh_v[256 * l:256 * l + 256, :] = jnp.where(
            lax.broadcasted_iota(jnp.int32, (256, two), 0) + 256 * l == target, 1.0, 0.0).astype(BF16)

    got(S_M1, m1rcv.at[pl.ds(0, 7)])
    m2snd[...] = jnp.sum(m1rcv[...], axis=0)
    for yy in y_peers:
        send(S_M2, m2snd, m2rcv.at[y], dev(yy, z, c, n))
    m2rcv[y] = m2snd[...]

    got(S_SCORE, arcv.at[pl.ds(0, 7)])
    halves = []
    for cs in range(NC):
        half = (arcv[4 * cs] + arcv[4 * cs + 1]) + (arcv[4 * cs + 2] + arcv[4 * cs + 3])
        for t in range(2):
            st_v[2 * cs + t] = half[:, 128 * t:128 * t + 128]
        halves.append(half)
    tiles = []
    for t in range(4):
        ordered = jnp.concatenate([st_v[t, pl.ds(0, 16, 2), :], st_v[t, pl.ds(1, 16, 2), :]], axis=0)
        tiles.append(jnp.concatenate([ordered] * 4, axis=0).T)
    s4 = jnp.concatenate(tiles, axis=0)
    hi = s4.astype(BF16)
    lo = (s4 - hi.astype(F32)).astype(BF16)
    packed = jnp.dot(oh_v[...], jnp.concatenate([hi, lo], axis=1), preferred_element_type=F32)
    lane_group = lax.broadcasted_iota(jnp.int32, (256, 128), 1) // SLICE
    slots = jnp.zeros((256, 128), F32)
    for l in range(4):
        piece = packed[256 * l:256 * l + 256, :]
        slots = jnp.where(lane_group == l, piece[:, :128] + piece[:, 128:], slots)
    for r in range(4):
        csnd[:, r, :] = slots[64 * r:64 * r + 64, :]
    first = jnp.sum(s4, axis=0, keepdims=True)
    second = jnp.sum(s4 * s4, axis=0, keepdims=True)
    stat = jnp.where(lax.broadcasted_iota(jnp.int32, (1, 128), 1) < SLICE, first, second)
    csnd[:, 4, :] = jnp.broadcast_to(stat, (CHIPS, 128))

    pl.semaphore_wait(plane_sem, len(y_peers))
    order = sorted(range(1, CHIPS), key=lambda j: -(min(j // 8, 8 - j // 8) + min(j % 8, 8 - j % 8)))
    for j in order:
        yy, zz = (y + j // 8) % NY, (z + j % 8) % NZ
        send(S_CHIP, csnd.at[yy * NZ + zz], crcv.at[chip], dev(yy, zz, c, n))
    crcv[chip] = csnd[chip]

    for cs in range(NC):
        bsnd[cs] = halves[cs].astype(BF16)
    for cc, nn in group_peers:
        send(S_BACK, bsnd.at[cc], brcv.at[me8], dev(y, z, cc, nn))
    brcv[me8] = bsnd[c]

    got(S_R1, r1rcv.at[pl.ds(0, 7)])
    here = r1rcv[:, 0, :]
    for yy in range(NY):
        r2snd[yy] = here if yy == 0 else pltpu.roll(here, 128 - 16 * yy, 1)
    for yy in y_peers:
        send(S_R2, r2snd.at[yy], r2rcv.at[y], dev(yy, z, c, n))
    r2rcv[y] = r2snd[y]

    got(S_M2, m2rcv.at[pl.ds(0, 7)])
    m3snd[...] = jnp.sum(m2rcv[...], axis=0)
    for cc, nn in group_peers:
        send(S_M3, m3snd, m3rcv.at[me8], dev(y, z, cc, nn))
    m3rcv[me8] = m3snd[...]

    got(S_MET_X, met_v.at[pl.ds(0, 3)])
    for dn in (1, 2, 3):
        blk = c * NX + (n + dn) % NX
        send(S_MET_C, met_v.at[blk], met_v.at[blk], dev(y, z, 1 - c, n))

    got(S_R2, r2rcv.at[pl.ds(0, 7)])
    rr = r2rcv[...].reshape(CHIPS, 128).astype(jnp.int32)
    spot = lax.broadcasted_iota(jnp.int32, (CHIPS, DIES_DEV), 1) + 1
    for cp in range(NC):
        for l in range(4):
            for cs in range(NC):
                s16 = (2 * cp + cs) * 4 + l
                ohr_v[cp, pl.ds(l * 128 + cs * 64, 64), :] = jnp.where(
                    rr[:, s16:s16 + 1] == spot, 1.0, 0.0).astype(BF16)

    got(S_M3, m3rcv.at[pl.ds(0, 7)])
    got(S_MET_C, met_v.at[pl.ds(0, 4)])
    for nn in range(NX):
        both = m3rcv[nn] + m3rcv[NX + nn]
        center = both[0:4, :] / TOTAL
        scaling = lax.rsqrt(both[4:8, :] / TOTAL - center * center + EPSILON)
        for cs in range(NC):
            blk = cs * NX + nn
            for t in range(4):
                span = slice(128 * t, 128 * t + 128)
                mz_v[blk, :, span] = (
                    (met_v[blk, :, span].astype(F32) - center[t:t + 1, :]) * scaling[t:t + 1, :]
                ).astype(BF16)

    got(S_CHIP, crcv.at[pl.ds(0, 63)])
    stat = jnp.sum(crcv[:, 4, :], axis=0, keepdims=True)
    lg = lax.broadcasted_iota(jnp.int32, (1, 128), 1) // SLICE
    s1 = jnp.where(lg == 0, stat, 0.0)
    s2 = jnp.where(lg == 1, stat, 0.0)
    s1 = s1 + pltpu.roll(s1, 32, 1)
    s1 = s1 + pltpu.roll(s1, 64, 1)
    s2 = s2 + pltpu.roll(s2, 32, 1)
    s2 = s2 + pltpu.roll(s2, 64, 1)
    center = s1 / TOTAL
    scaling = lax.rsqrt(s2 / TOTAL - center * center + EPSILON)
    zf = jnp.concatenate([(crcv[:, r, :] - center) * scaling for r in range(4)], axis=0)
    zt = zf.T.astype(BF16)
    placed = []
    for cp in range(NC):
        lhs = jnp.concatenate([zt[32 * l:32 * l + 32, 128 * cp:128 * cp + 128] for l in range(4)], axis=1)
        placed.append(jnp.dot(lhs, ohr_v[cp], preferred_element_type=F32).astype(BF16))
    for nn in range(NX):
        cross = jnp.dot(placed[0], mz_v[nn], preferred_element_type=F32) + jnp.dot(
            placed[1], mz_v[NX + nn], preferred_element_type=F32)
        for t in range(4):
            for kk in range(2):
                dsnd[pl.ds(nn * 8 + t * 2 + kk, 16, 32), :] = cross[16 * kk:16 * kk + 16, 128 * t:128 * t + 128]

    mine = (c * NX + n + y) % NZ == z
    for dy in FAR + (0,):
        yy = (y + dy) % NY
        zz = (me8 + yy) % NZ
        for dc, dn in ((0, 2), (1, 2), (0, 1), (1, 1), (0, 3), (1, 3), (1, 0), (0, 0)):
            cc, nn = (c + dc) % NC, (n + dn) % NX
            src = dsnd.at[pl.ds(pl.multiple_of(((yy * 2 + cc) * 4 + nn) * 8, 8), 8), :]
            if (dy, dc, dn) == (0, 0, 0):
                @pl.when(jnp.logical_not(mine))
                def _():
                    send(S_OUT, src, drcv.at[chip], dev(yy, zz, cc, nn))

                @pl.when(mine)
                def _():
                    pltpu.make_async_copy(src, drcv.at[chip], rsem.at[S_OUT]).start()
            else:
                send(S_OUT, src, drcv.at[chip], dev(yy, zz, cc, nn))

    got(S_BACK, brcv.at[pl.ds(0, 7)])
    slot_k = lax.broadcasted_iota(jnp.int32, (COMP, COMP), 1)
    q_of, y_of, rest = slot_k // 32, (slot_k // 4) % 8, slot_k % 4
    natural = 32 * y_of + 4 * ((q_of + y_of) % 8) + rest
    perm = jnp.where(lax.broadcasted_iota(jnp.int32, (COMP, COMP), 0) == natural, 1.0, 0.0).astype(BF16)
    score_t = jnp.dot(perm, brcv[...].reshape(COMP, DIES_DEV), preferred_element_type=F32)
    score = score_t.T.astype(BF16)
    acc = jnp.zeros((DIES_DEV, 128), F32)
    for j in range(CHUNKS):
        span = pl.ds(j * step, step)
        rebuilt = lax.dot_general(
            score, load_v[span, :], (((1,), (1,)), ((), ())), preferred_element_type=F32)
        residue = cen_v[:, span].astype(F32) - rebuilt
        residue = residue * residue
        for t in range(step // 128):
            acc = acc + residue[:, 128 * t:128 * t + 128]
    line = jnp.sum(acc.T, axis=0, keepdims=True) / (FEAT * NX)
    esnd[0:1, :] = line[:, :128]
    esnd[1:2, :] = line[:, 128:]
    for dn in (2, 1, 3):
        send(S_RES, esnd, ercv.at[n], dev(y, z, c, (n + dn) % NX))
    ercv[n] = esnd[...]
    got(S_RES, ercv.at[pl.ds(0, 3)])
    total = (ercv[0] + ercv[1]) + (ercv[2] + ercv[3])
    pick = jnp.where(n >= 2, total[1:2, :], total[0:1, :])
    res_out[...] = jnp.where(n % 2 == 1, pick[:, 64:], pick[:, :64])

    got(S_OUT, drcv)
    out = jnp.sum(drcv[...], axis=0) * (1.0 / math.sqrt(TOTAL))
    for t in range(4):
        cross_out[:, 128 * t:128 * t + 128] = out[2 * t:2 * t + 2, :]

    sent(S_SCORE, asnd.at[pl.ds(0, 7)])
    sent(S_ROUTE, route_v.at[0])
    for _ in range(7):
        sent(S_M1, m1snd)
        sent(S_M2, m2snd)
        sent(S_M3, m3snd)
    sent(S_MET_X, met_v.at[pl.ds(0, 3)])
    sent(S_MET_C, met_v.at[pl.ds(0, 4)])
    sent(S_R1, r1snd.at[pl.ds(0, 7)])
    sent(S_R2, r2snd.at[pl.ds(0, 7)])
    sent(S_CHIP, csnd.at[pl.ds(0, 63)])
    sent(S_BACK, brcv.at[pl.ds(0, 7)])
    sent(S_RES, ercv.at[pl.ds(0, 3)])
    sent(S_OUT, drcv.at[pl.ds(0, 63)])

    @pl.when(jnp.logical_not(mine))
    def _():
        sent(S_OUT, drcv.at[0])


def shards(iv_curves, mean_curve, loadings, metrology, dest_owner, dest_row):
    any_spec = pl.BlockSpec(memory_space=pl.ANY)
    vmem_spec = pl.BlockSpec(memory_space=pltpu.VMEM)
    scratch = [
        pltpu.VMEM((DIES_DEV, FEAT), BF16),
        pltpu.VMEM((1, FEAT), F32),
        pltpu.VMEM((FEAT, COMP), BF16),
        pltpu.VMEM((DIES_DEV, FEAT), BF16),
        pltpu.VMEM((COMP, DIES_DEV), F32),
        pltpu.VMEM((GROUP, DIES_DEV, METRO), BF16),
        pltpu.VMEM((GROUP, DIES_DEV, METRO), BF16),
        pltpu.VMEM((NC, 2, 2, 128), jnp.int32),
        pltpu.VMEM((GROUP, SLICE, DIES_DEV), F32),
        pltpu.VMEM((GROUP, SLICE, DIES_DEV), F32),
        pltpu.VMEM((4, SLICE, 128), F32),
        pltpu.VMEM((NC, SLICE, DIES_DEV), BF16),
        pltpu.VMEM((GROUP, SLICE, DIES_DEV), BF16),
        pltpu.VMEM((1024, NC * DIES_DEV), BF16),
        pltpu.VMEM((NC, 512, DIES_DEV), BF16),
        pltpu.VMEM((CHIPS, 5, 128), F32),
        pltpu.VMEM((CHIPS, 5, 128), F32),
        pltpu.VMEM((CHIPS * 8, 128), F32),
        pltpu.VMEM((CHIPS, 8, 128), F32),
        pltpu.VMEM((8, 128), F32),
        pltpu.VMEM((NZ, 8, 128), F32),
        pltpu.VMEM((8, 128), F32),
        pltpu.VMEM((NY, 8, 128), F32),
        pltpu.VMEM((8, 128), F32),
        pltpu.VMEM((GROUP, 8, 128), F32),
        pltpu.VMEM((NZ, 1, 128), F32),
        pltpu.VMEM((NZ, 1, 128), F32),
        pltpu.VMEM((NY, 8, 128), F32),
        pltpu.VMEM((NY, 8, 128), F32),
        pltpu.VMEM((2, 128), F32),
        pltpu.VMEM((NX, 2, 128), F32),
        pltpu.SemaphoreType.DMA((2 * CHUNKS + 4,)),
        pltpu.SemaphoreType.DMA((N_SEM,)),
        pltpu.SemaphoreType.DMA((N_SEM,)),
        pltpu.SemaphoreType.REGULAR,
    ]
    residual, cross = pl.pallas_call(
        body,
        out_shape=(
            jax.ShapeDtypeStruct((1, DIES_DEV // NX), F32),
            jax.ShapeDtypeStruct((2, METRO), F32),
        ),
        in_specs=[any_spec] * 6,
        out_specs=(vmem_spec, vmem_spec),
        scratch_shapes=scratch,
        compiler_params=pltpu.CompilerParams(
            collective_id=1, has_side_effects=True, vmem_limit_bytes=40 * 2**20),
        cost_estimate=pl.CostEstimate(flops=10**9, bytes_accessed=3 * 10**6, transcendentals=0),
    )(
        iv_curves,
        mean_curve.reshape(1, FEAT),
        loadings,
        metrology,
        dest_owner.reshape(2, 128),
        dest_row.reshape(2, 128),
    )
    return residual.reshape(DIES_DEV // NX), cross


def solution(mesh):
    in_specs = (
        P("wide", "narrow"),
        P("narrow"),
        P("narrow", None),
        P("wide", "narrow"),
        P("wide"),
        P("wide"),
    )
    out_specs = (P(("wide", "narrow")), P("wide", "narrow"))
    return jax.shard_map(shards, mesh=mesh, in_specs=in_specs, out_specs=out_specs, check_vma=False)
```

time: 544 us -> 57.8 us (0.11)
  the two profiles are of different devices: /device:TPU:24 before, /device:TPU:1 now
where the time goes in v1:
time: 57.8 us; the launch traced here: 57.5 us
  Pallas kernels  51 us (88%)
  local copies, waits for them, and re-layouts  5.88 us (10%)
  between operations  0.66 us (1%)
    pallas_call x1, Pallas kernels, shards(): pl.pallas_call(body, out_shape=(jax.ShapeDtypeStruct((1, DIES_DEV // NX),...  51 us
    unnamed x14, local copies, waits for them, and re-layouts  5.88 us

profile of v1, /device:TPU:1, one launch (start us, length us, event | category | flops | bytes accessed | tf_op | source)
XLA Modules:
  0.0 57.5 jit_solution(13498540897312701252)
XLA Ops:
  0.6 0.0 copy-start.5
  0.6 0.0 copy-start.4
  0.7 0.7 %copy-done.5 = s32[256]{0:T(256)S(1)} copy-done((s32[256]{0:T(256)S(1)}, s32[256]{0:T(256)}, u32[]{:S(2)}) %copy-start.5) | copy-done | bytes 1048
  1.3 0.0 copy-done.4
  1.3 0.0 copy-start
  1.3 1.2 %copy-done = bf16[256,2048]{1,0:T(8,128)(2,1)S(1)} copy-done((bf16[256,2048]{1,0:T(8,128)(2,1)S(1)}, bf16[256,2048]{1,0:T(8,128)(2,1)}, u32[]{:S(2)}) %copy-start) | copy-done | bytes 1048600
  2.6 0.0 copy-start.1
  2.6 1.2 %copy-done.1 = bf16[2048,256]{1,0:T(8,128)(2,1)S(1)} copy-done((bf16[2048,256]{1,0:T(8,128)(2,1)S(1)}, bf16[2048,256]{1,0:T(8,128)(2,1)}, u32[]{:S(2)}) %copy-start.1) | copy-done | bytes 1048600
  3.8 0.0 copy-start.2
  3.8 0.9 %copy-done.2 = bf16[256,512]{1,0:T(8,128)(2,1)S(1)} copy-done((bf16[256,512]{1,0:T(8,128)(2,1)S(1)}, bf16[256,512]{1,0:T(8,128)(2,1)}, u32[]{:S(2)}) %copy-start.2) | copy-done | bytes 262168
  4.7 0.0 copy-start.3
  4.7 0.7 %copy-done.3 = f32[2048]{0:T(1024)S(1)} copy-done((f32[2048]{0:T(1024)S(1)}, f32[2048]{0:T(1024)}, u32[]{:S(2)}) %copy-start.3) | copy-done | bytes 8216
  5.4 51.0 %shard_map.77 = (f32[1,64]{1,0:T(1,128)S(1)}, f32[2,512]{1,0:T(2,128)S(1)}) custom-call(bf16[256,2048]{1,0:T(8,128)(2,1)S(1)} %copy-done, f32[1,2048]{1,0:T(1,128)S(1)} %bitcast.4, bf16[2048,256]{1,0:T(8,128)(2,1)S(1)} %copy-done.1, bf16[256,512]{1,0:T(8,128)(2,1)S(1)} %copy-done.2, s32[2,128]{1,0:T(2,128)S(1)} %bitcast.5, s32[2,128]{1,0:T(2,128)S(1)} %bitcast.6), custom_call_target="tpu_custom_call" | custom-call | flops 1000000000 | bytes 3000000 | tf_op jit(solution)/shard_map/pallas_call | solution.py:391
  56.4 0.5 copy.10
  56.9 0.6 %copy.11 = f32[2,512]{1,0:T(2,128)} copy(f32[2,512]{1,0:T(2,128)S(1)} %get-tuple-element.9) | data formatting | bytes 8192
Async XLA Ops:
  0.6 0.7 %copy-start.5 = (s32[256]{0:T(256)S(1)}, s32[256]{0:T(256)}, u32[]{:S(2)}) copy-start(s32[256]{0:T(256)} %param.11) | copy-start | bytes 3076
  0.6 0.7 %copy-start.4 = (s32[256]{0:T(256)S(1)}, s32[256]{0:T(256)}, u32[]{:S(2)}) copy-start(s32[256]{0:T(256)} %param.10) | copy-start | bytes 3076
  1.3 1.2 %copy-start = (bf16[256,2048]{1,0:T(8,128)(2,1)S(1)}, bf16[256,2048]{1,0:T(8,128)(2,1)}, u32[]{:S(2)}) copy-start(bf16[256,2048]{1,0:T(8,128)(2,1)} %iv_hbm.1) | copy-start | bytes 3145732
  2.6 1.2 %copy-start.1 = (bf16[2048,256]{1,0:T(8,128)(2,1)S(1)}, bf16[2048,256]{1,0:T(8,128)(2,1)}, u32[]{:S(2)}) copy-start(bf16[2048,256]{1,0:T(8,128)(2,1)} %load_hbm.1) | copy-start | bytes 3145732
  3.8 0.9 %copy-start.2 = (bf16[256,512]{1,0:T(8,128)(2,1)S(1)}, bf16[256,512]{1,0:T(8,128)(2,1)}, u32[]{:S(2)}) copy-start(bf16[256,512]{1,0:T(8,128)(2,1)} %met_hbm.1) | copy-start | bytes 786436
  4.7 0.7 %copy-start.3 = (f32[2048]{0:T(1024)S(1)}, f32[2048]{0:T(1024)}, u32[]{:S(2)}) copy-start(f32[2048]{0:T(1024)} %param.7) | copy-start | bytes 24580

commit v2 on v1

--- a/solution.py
+++ b/solution.py
@@ -24,7 +24,7 @@
 TOTAL = DIES_DEV * CHIPS * NC
 CHUNKS = 4
 FAR = (4, 3, 5, 2, 6, 1, 7)
-(S_ROUTE, S_SCORE, S_MET_X, S_MET_C, S_M1, S_M2, S_M3, S_R1, S_R2, S_CHIP, S_BACK, S_RES, S_OUT) = range(13)
+(S_ROUTE, S_SCORE, S_MET, S_M1, S_M2, S_M3, S_R1, S_R2, S_CHIP, S_PLACED, S_BACK, S_RES, S_OUT) = range(13)
 N_SEM = 13
 
 
@@ -32,8 +32,8 @@
     iv_hbm, mean_hbm, load_hbm, met_hbm, own_hbm, row_hbm,
     res_out, cross_out,
     iv_v, mean_v, load_v, cen_v, pt_v, met_v, mz_v, route_v,
-    asnd, arcv, st_v, bsnd, brcv, oh_v, ohr_v,
-    csnd, crcv, dsnd, drcv,
+    asnd, arcv, bsnd, brcv, oh_v, ohr_v,
+    csnd, crcv, placed_v, dsnd, drcv,
     m1snd, m1rcv, m2snd, m2rcv, m3snd, m3rcv,
     r1snd, r1rcv, r2snd, r2rcv, esnd, ercv,
     ld_sem, ssem, rsem, plane_sem,
@@ -72,7 +72,7 @@
             pltpu.make_async_copy(load_hbm.at[span], load_v.at[span], ld_sem.at[2 * j + 1]),
         ))
     mean_load = pltpu.make_async_copy(mean_hbm, mean_v, ld_sem.at[2 * CHUNKS])
-    met_load = pltpu.make_async_copy(met_hbm, met_v.at[me8], ld_sem.at[2 * CHUNKS + 1])
+    met_load = pltpu.make_async_copy(met_hbm, met_v.at[c], ld_sem.at[2 * CHUNKS + 1])
     own_load = pltpu.make_async_copy(own_hbm, route_v.at[c, 0], ld_sem.at[2 * CHUNKS + 2])
     row_load = pltpu.make_async_copy(row_hbm, route_v.at[c, 1], ld_sem.at[2 * CHUNKS + 3])
     mean_load.start()
@@ -100,13 +100,18 @@
         cen = (iv_v[:, span].astype(F32) - mean_v[:, span]).astype(BF16)
         cen_v[:, span] = cen
         part = part + jnp.dot(cen, load_v[span, :], preferred_element_type=F32)
-    pt_v[...] = part.T
-    for q in range(GROUP):
-        for yy in range(NY):
-            asnd[q, 4 * yy:4 * yy + 4, :] = pt_v[pl.ds(32 * yy + 4 * ((q + yy) % NZ), 4), :]
+    part_t = part.T
+    for t in range(2):
+        pt_v[t] = part_t[:, 128 * t:128 * t + 128]
+    for cc in range(NC):
+        for nn in range(NX):
+            for kk in range(2):
+                for t in range(2):
+                    asnd[cc * NX + nn, 16 * kk:16 * kk + 16, 128 * t:128 * t + 128] = pt_v[
+                        t, pl.ds(64 * nn + 2 * cc + kk, 16, 4), :]
 
     met_load.wait()
-    met = met_v[me8].astype(F32)
+    met = met_v[c].astype(F32)
     tot = jnp.sum(met, axis=0, keepdims=True)
     sq = jnp.sum(met * met, axis=0, keepdims=True)
     for t in range(4):
@@ -125,9 +130,7 @@
         send(S_M1, m1snd, m1rcv.at[z], dev(y, zz, c, n))
     for yy in y_peers:
         pl.semaphore_signal(plane_sem, inc=1, device_id=dev(yy, z, c, n), device_id_type=MESH)
-    for dn in (2, 1, 3):
-        send(S_MET_X, met_v.at[me8], met_v.at[me8], dev(y, z, c, (n + dn) % NX))
-    send(S_MET_C, met_v.at[me8], met_v.at[me8], dev(y, z, 1 - c, n))
+    send(S_MET, met_v.at[c], met_v.at[c], dev(y, z, 1 - c, n))
     arcv[me8] = asnd[me8]
     m1rcv[z] = m1snd[...]
 
@@ -175,14 +178,8 @@
     halves = []
     for cs in range(NC):
         half = (arcv[4 * cs] + arcv[4 * cs + 1]) + (arcv[4 * cs + 2] + arcv[4 * cs + 3])
-        for t in range(2):
-            st_v[2 * cs + t] = half[:, 128 * t:128 * t + 128]
         halves.append(half)
-    tiles = []
-    for t in range(4):
-        ordered = jnp.concatenate([st_v[t, pl.ds(0, 16, 2), :], st_v[t, pl.ds(1, 16, 2), :]], axis=0)
-        tiles.append(jnp.concatenate([ordered] * 4, axis=0).T)
-    s4 = jnp.concatenate(tiles, axis=0)
+    s4 = jnp.concatenate([jnp.concatenate([half] * 4, axis=0).T for half in halves], axis=0)
     hi = s4.astype(BF16)
     lo = (s4 - hi.astype(F32)).astype(BF16)
     packed = jnp.dot(oh_v[...], jnp.concatenate([hi, lo], axis=1), preferred_element_type=F32)
@@ -221,14 +218,8 @@
 
     got(S_M2, m2rcv.at[pl.ds(0, 7)])
     m3snd[...] = jnp.sum(m2rcv[...], axis=0)
-    for cc, nn in group_peers:
-        send(S_M3, m3snd, m3rcv.at[me8], dev(y, z, cc, nn))
-    m3rcv[me8] = m3snd[...]
-
-    got(S_MET_X, met_v.at[pl.ds(0, 3)])
-    for dn in (1, 2, 3):
-        blk = c * NX + (n + dn) % NX
-        send(S_MET_C, met_v.at[blk], met_v.at[blk], dev(y, z, 1 - c, n))
+    send(S_M3, m3snd, m3rcv.at[c], dev(y, z, 1 - c, n))
+    m3rcv[c] = m3snd[...]
 
     got(S_R2, r2rcv.at[pl.ds(0, 7)])
     rr = r2rcv[...].reshape(CHIPS, 128).astype(jnp.int32)
@@ -240,19 +231,17 @@
                 ohr_v[cp, pl.ds(l * 128 + cs * 64, 64), :] = jnp.where(
                     rr[:, s16:s16 + 1] == spot, 1.0, 0.0).astype(BF16)
 
-    got(S_M3, m3rcv.at[pl.ds(0, 7)])
-    got(S_MET_C, met_v.at[pl.ds(0, 4)])
-    for nn in range(NX):
-        both = m3rcv[nn] + m3rcv[NX + nn]
-        center = both[0:4, :] / TOTAL
-        scaling = lax.rsqrt(both[4:8, :] / TOTAL - center * center + EPSILON)
-        for cs in range(NC):
-            blk = cs * NX + nn
-            for t in range(4):
-                span = slice(128 * t, 128 * t + 128)
-                mz_v[blk, :, span] = (
-                    (met_v[blk, :, span].astype(F32) - center[t:t + 1, :]) * scaling[t:t + 1, :]
-                ).astype(BF16)
+    got(S_M3, m3rcv.at[0])
+    got(S_MET, met_v.at[0])
+    both = m3rcv[0] + m3rcv[1]
+    center = both[0:4, :] / TOTAL
+    scaling = lax.rsqrt(both[4:8, :] / TOTAL - center * center + EPSILON)
+    for cs in range(NC):
+        for t in range(4):
+            span = slice(128 * t, 128 * t + 128)
+            mz_v[256 * cs:256 * cs + 256, span] = (
+                (met_v[cs, :, span].astype(F32) - center[t:t + 1, :]) * scaling[t:t + 1, :]
+            ).astype(BF16)
 
     got(S_CHIP, crcv.at[pl.ds(0, 63)])
     stat = jnp.sum(crcv[:, 4, :], axis=0, keepdims=True)
@@ -267,39 +256,31 @@
     scaling = lax.rsqrt(s2 / TOTAL - center * center + EPSILON)
     zf = jnp.concatenate([(crcv[:, r, :] - center) * scaling for r in range(4)], axis=0)
     zt = zf.T.astype(BF16)
-    placed = []
     for cp in range(NC):
         lhs = jnp.concatenate([zt[32 * l:32 * l + 32, 128 * cp:128 * cp + 128] for l in range(4)], axis=1)
-        placed.append(jnp.dot(lhs, ohr_v[cp], preferred_element_type=F32).astype(BF16))
+        placed_v[n, :, 256 * cp:256 * cp + 256] = jnp.dot(
+            lhs, ohr_v[cp], preferred_element_type=F32).astype(BF16)
+
+    for dn in (2, 1, 3):
+        send(S_PLACED, placed_v.at[n], placed_v.at[n], dev(y, z, c, (n + dn) % NX))
+    got(S_PLACED, placed_v.at[pl.ds(0, 3)])
+    cross = jnp.dot(placed_v[...].reshape(4 * SLICE, NC * DIES_DEV), mz_v[...], preferred_element_type=F32)
     for nn in range(NX):
-        cross = jnp.dot(placed[0], mz_v[nn], preferred_element_type=F32) + jnp.dot(
-            placed[1], mz_v[NX + nn], preferred_element_type=F32)
-        for t in range(4):
-            for kk in range(2):
-                dsnd[pl.ds(nn * 8 + t * 2 + kk, 16, 32), :] = cross[16 * kk:16 * kk + 16, 128 * t:128 * t + 128]
-
-    mine = (c * NX + n + y) % NZ == z
-    for dy in FAR + (0,):
-        yy = (y + dy) % NY
-        zz = (me8 + yy) % NZ
-        for dc, dn in ((0, 2), (1, 2), (0, 1), (1, 1), (0, 3), (1, 3), (1, 0), (0, 0)):
-            cc, nn = (c + dc) % NC, (n + dn) % NX
-            src = dsnd.at[pl.ds(pl.multiple_of(((yy * 2 + cc) * 4 + nn) * 8, 8), 8), :]
-            if (dy, dc, dn) == (0, 0, 0):
-                @pl.when(jnp.logical_not(mine))
-                def _():
-                    send(S_OUT, src, drcv.at[chip], dev(yy, zz, cc, nn))
-
-                @pl.when(mine)
-                def _():
-                    pltpu.make_async_copy(src, drcv.at[chip], rsem.at[S_OUT]).start()
-            else:
-                send(S_OUT, src, drcv.at[chip], dev(yy, zz, cc, nn))
+        for kk in range(2):
+            for t in range(4):
+                base = 32 * nn + 16 * kk
+                dsnd[pl.ds(128 * nn + t * 2 + kk, 16, 8), :] = cross[base:base + 16, 128 * t:128 * t + 128]
+
+    for j in order:
+        yy, zz = (y + j // 8) % NY, (z + j % 8) % NZ
+        block = pl.ds(pl.multiple_of((yy * NZ + zz) * 8, 8), 8)
+        send(S_OUT, dsnd.at[block, :], drcv.at[chip], dev(yy, zz, c, n))
+    drcv[chip] = dsnd[pl.ds(pl.multiple_of(chip * 8, 8), 8), :]
 
     got(S_BACK, brcv.at[pl.ds(0, 7)])
     slot_k = lax.broadcasted_iota(jnp.int32, (COMP, COMP), 1)
-    q_of, y_of, rest = slot_k // 32, (slot_k // 4) % 8, slot_k % 4
-    natural = 32 * y_of + 4 * ((q_of + y_of) % 8) + rest
+    c_of, n_of, kk_of, i_of = slot_k // 128, (slot_k // 32) % 4, (slot_k // 16) % 2, slot_k % 16
+    natural = 64 * n_of + 4 * i_of + 2 * c_of + kk_of
     perm = jnp.where(lax.broadcasted_iota(jnp.int32, (COMP, COMP), 0) == natural, 1.0, 0.0).astype(BF16)
     score_t = jnp.dot(perm, brcv[...].reshape(COMP, DIES_DEV), preferred_element_type=F32)
     score = score_t.T.astype(BF16)
@@ -323,7 +304,7 @@
     pick = jnp.where(n >= 2, total[1:2, :], total[0:1, :])
     res_out[...] = jnp.where(n % 2 == 1, pick[:, 64:], pick[:, :64])
 
-    got(S_OUT, drcv)
+    got(S_OUT, drcv.at[pl.ds(0, 63)])
     out = jnp.sum(drcv[...], axis=0) * (1.0 / math.sqrt(TOTAL))
     for t in range(4):
         cross_out[:, 128 * t:128 * t + 128] = out[2 * t:2 * t + 2, :]
@@ -333,19 +314,15 @@
     for _ in range(7):
         sent(S_M1, m1snd)
         sent(S_M2, m2snd)
-        sent(S_M3, m3snd)
-    sent(S_MET_X, met_v.at[pl.ds(0, 3)])
-    sent(S_MET_C, met_v.at[pl.ds(0, 4)])
+    sent(S_M3, m3snd)
+    sent(S_MET, met_v.at[0])
+    sent(S_PLACED, placed_v.at[pl.ds(0, 3)])
     sent(S_R1, r1snd.at[pl.ds(0, 7)])
     sent(S_R2, r2snd.at[pl.ds(0, 7)])
     sent(S_CHIP, csnd.at[pl.ds(0, 63)])
     sent(S_BACK, brcv.at[pl.ds(0, 7)])
     sent(S_RES, ercv.at[pl.ds(0, 3)])
     sent(S_OUT, drcv.at[pl.ds(0, 63)])
-
-    @pl.when(jnp.logical_not(mine))
-    def _():
-        sent(S_OUT, drcv.at[0])
 
 
 def shards(iv_curves, mean_curve, loadings, metrology, dest_owner, dest_row):
@@ -356,19 +333,19 @@
         pltpu.VMEM((1, FEAT), F32),
         pltpu.VMEM((FEAT, COMP), BF16),
         pltpu.VMEM((DIES_DEV, FEAT), BF16),
-        pltpu.VMEM((COMP, DIES_DEV), F32),
-        pltpu.VMEM((GROUP, DIES_DEV, METRO), BF16),
-        pltpu.VMEM((GROUP, DIES_DEV, METRO), BF16),
+        pltpu.VMEM((2, COMP, 128), F32),
+        pltpu.VMEM((NC, DIES_DEV, METRO), BF16),
+        pltpu.VMEM((NC * DIES_DEV, METRO), BF16),
         pltpu.VMEM((NC, 2, 2, 128), jnp.int32),
         pltpu.VMEM((GROUP, SLICE, DIES_DEV), F32),
         pltpu.VMEM((GROUP, SLICE, DIES_DEV), F32),
-        pltpu.VMEM((4, SLICE, 128), F32),
         pltpu.VMEM((NC, SLICE, DIES_DEV), BF16),
         pltpu.VMEM((GROUP, SLICE, DIES_DEV), BF16),
         pltpu.VMEM((1024, NC * DIES_DEV), BF16),
         pltpu.VMEM((NC, 512, DIES_DEV), BF16),
         pltpu.VMEM((CHIPS, 5, 128), F32),
         pltpu.VMEM((CHIPS, 5, 128), F32),
+        pltpu.VMEM((NX, SLICE, NC * DIES_DEV), BF16),
         pltpu.VMEM((CHIPS * 8, 128), F32),
         pltpu.VMEM((CHIPS, 8, 128), F32),
         pltpu.VMEM((8, 128), F32),
@@ -376,7 +353,7 @@
         pltpu.VMEM((8, 128), F32),
         pltpu.VMEM((NY, 8, 128), F32),
         pltpu.VMEM((8, 128), F32),
-        pltpu.VMEM((GROUP, 8, 128), F32),
+        pltpu.VMEM((NC, 8, 128), F32),
         pltpu.VMEM((NZ, 1, 128), F32),
         pltpu.VMEM((NZ, 1, 128), F32),
         pltpu.VMEM((NY, 8, 128), F32),
@@ -398,7 +375,7 @@
         out_specs=(vmem_spec, vmem_spec),
         scratch_shapes=scratch,
         compiler_params=pltpu.CompilerParams(
-            collective_id=1, has_side_effects=True, vmem_limit_bytes=40 * 2**20),
+            collective_id=1, has_side_effects=True, vmem_limit_bytes=63 * 2**20),
         cost_estimate=pl.CostEstimate(flops=10**9, bytes_accessed=3 * 10**6, transcendentals=0),
     )(
         iv_curves,

time: 57.8 us -> 44 us (0.76)
  the two profiles are of different devices: /device:TPU:1 before, /device:TPU:2 now
where the time goes in v2:
time: 44 us; the launch traced here: 43.8 us
  Pallas kernels  41.4 us (94%)
  local copies, waits for them, and re-layouts  1.74 us (4%)
  between operations  0.66 us (2%)
    pallas_call x1, Pallas kernels, shards(): pl.pallas_call(body, out_shape=(jax.ShapeDtypeStruct((1, DIES_DEV // NX),...  41.4 us
    unnamed x6, local copies, waits for them, and re-layouts  1.74 us

profile of v2, /device:TPU:2, one launch (start us, length us, event | category | flops | bytes accessed | tf_op | source)
XLA Modules:
  0.0 43.8 jit_solution(17316204856500608200)
XLA Ops:
  0.6 41.4 %shard_map.77 = (f32[1,64]{1,0:T(1,128)}, f32[2,512]{1,0:T(2,128)}) custom-call(bf16[256,2048]{1,0:T(8,128)(2,1)} %iv_hbm.1, f32[1,2048]{1,0:T(1,128)} %bitcast.4, bf16[2048,256]{1,0:T(8,128)(2,1)} %load_hbm.1, bf16[256,512]{1,0:T(8,128)(2,1)} %met_hbm.1, s32[2,128]{1,0:T(2,128)} %bitcast.5, s32[2,128]{1,0:T(2,128)} %bitcast.6), custom_call_target="tpu_custom_call" | custom-call | flops 1000000000 | bytes 3000000 | tf_op jit(solution)/shard_map/pallas_call | solution.py:368
  42.1 0.0 copy-start
  42.1 0.0 copy-start.1
  42.1 0.6 %copy-done.1 = f32[1,64]{1,0:T(1,128)S(1)} copy-done((f32[1,64]{1,0:T(1,128)S(1)}, f32[1,64]{1,0:T(1,128)}, u32[]{:S(2)}) %copy-start.1) | copy-done | bytes 280
  42.7 0.5 %copy.10 = f32[64]{0:T(128)} copy(f32[64]{0:T(128)S(1)} %bitcast.7) | data formatting | bytes 512
  43.2 0.0 copy-done
  43.2 0.6 %copy.11 = f32[2,512]{1,0:T(2,128)} copy(f32[2,512]{1,0:T(2,128)S(1)} %copy-done) | data formatting | bytes 8192
Async XLA Ops:
  42.1 1.2 %copy-start = (f32[2,512]{1,0:T(2,128)S(1)}, f32[2,512]{1,0:T(2,128)}, u32[]{:S(2)}) copy-start(f32[2,512]{1,0:T(2,128)} %get-tuple-element.9) | copy-start | bytes 12292
  42.1 0.6 %copy-start.1 = (f32[1,64]{1,0:T(1,128)S(1)}, f32[1,64]{1,0:T(1,128)}, u32[]{:S(2)}) copy-start(f32[1,64]{1,0:T(1,128)} %get-tuple-element.4) | copy-start | bytes 772

commit v3 on v2

--- a/solution.py
+++ b/solution.py
@@ -79,9 +79,6 @@
     for a, b in loads:
         a.start()
         b.start()
-    met_load.start()
-    own_load.start()
-    row_load.start()
 
     barrier = pltpu.get_barrier_semaphore()
     for zz in z_peers:
@@ -90,6 +87,10 @@
         pl.semaphore_signal(barrier, inc=1, device_id=dev(yy, z, c, n), device_id_type=MESH)
     for cc, nn in group_peers:
         pl.semaphore_signal(barrier, inc=1, device_id=dev(y, z, cc, nn), device_id_type=MESH)
+
+    met_load.start()
+    own_load.start()
+    row_load.start()
 
     mean_load.wait()
     part = jnp.zeros((DIES_DEV, COMP), F32)
@@ -100,6 +101,8 @@
         cen = (iv_v[:, span].astype(F32) - mean_v[:, span]).astype(BF16)
         cen_v[:, span] = cen
         part = part + jnp.dot(cen, load_v[span, :], preferred_element_type=F32)
+    lead = part[0:1, :].astype(BF16).astype(F32)
+    part = jnp.where(lax.broadcasted_iota(jnp.int32, (DIES_DEV, COMP), 0) == 0, lead, part - lead)
     part_t = part.T
     for t in range(2):
         pt_v[t] = part_t[:, 128 * t:128 * t + 128]
@@ -108,7 +111,15 @@
             for kk in range(2):
                 for t in range(2):
                     asnd[cc * NX + nn, 16 * kk:16 * kk + 16, 128 * t:128 * t + 128] = pt_v[
-                        t, pl.ds(64 * nn + 2 * cc + kk, 16, 4), :]
+                        t, pl.ds(64 * nn + 2 * cc + kk, 16, 4), :].astype(BF16)
+
+    pl.semaphore_wait(barrier, len(z_peers) + len(y_peers) + len(group_peers))
+
+    for cc, nn in group_peers:
+        q = cc * NX + nn
+        send(S_SCORE, asnd.at[q], arcv.at[me8], dev(y, z, cc, nn))
+    for yy in y_peers:
+        pl.semaphore_signal(plane_sem, inc=1, device_id=dev(yy, z, c, n), device_id_type=MESH)
 
     met_load.wait()
     met = met_v[c].astype(F32)
@@ -120,16 +131,9 @@
     own_load.wait()
     row_load.wait()
 
-    pl.semaphore_wait(barrier, len(z_peers) + len(y_peers) + len(group_peers))
-
-    for cc, nn in group_peers:
-        q = cc * NX + nn
-        send(S_SCORE, asnd.at[q], arcv.at[me8], dev(y, z, cc, nn))
     send(S_ROUTE, route_v.at[c], route_v.at[c], dev(y, z, 1 - c, n))
     for zz in z_peers:
         send(S_M1, m1snd, m1rcv.at[z], dev(y, zz, c, n))
-    for yy in y_peers:
-        pl.semaphore_signal(plane_sem, inc=1, device_id=dev(yy, z, c, n), device_id_type=MESH)
     send(S_MET, met_v.at[c], met_v.at[c], dev(y, z, 1 - c, n))
     arcv[me8] = asnd[me8]
     m1rcv[z] = m1snd[...]
@@ -177,8 +181,9 @@
     got(S_SCORE, arcv.at[pl.ds(0, 7)])
     halves = []
     for cs in range(NC):
-        half = (arcv[4 * cs] + arcv[4 * cs + 1]) + (arcv[4 * cs + 2] + arcv[4 * cs + 3])
-        halves.append(half)
+        half = (arcv[4 * cs].astype(F32) + arcv[4 * cs + 1].astype(F32)) + (arcv[4 * cs + 2].astype(F32) + arcv[4 * cs + 3].astype(F32))
+        lead = jnp.where(lax.broadcasted_iota(jnp.int32, half.shape, 1) == 0, 0.0, half[:, 0:1])
+        halves.append(half + lead)
     s4 = jnp.concatenate([jnp.concatenate([half] * 4, axis=0).T for half in halves], axis=0)
     hi = s4.astype(BF16)
     lo = (s4 - hi.astype(F32)).astype(BF16)
@@ -263,19 +268,6 @@
 
     for dn in (2, 1, 3):
         send(S_PLACED, placed_v.at[n], placed_v.at[n], dev(y, z, c, (n + dn) % NX))
-    got(S_PLACED, placed_v.at[pl.ds(0, 3)])
-    cross = jnp.dot(placed_v[...].reshape(4 * SLICE, NC * DIES_DEV), mz_v[...], preferred_element_type=F32)
-    for nn in range(NX):
-        for kk in range(2):
-            for t in range(4):
-                base = 32 * nn + 16 * kk
-                dsnd[pl.ds(128 * nn + t * 2 + kk, 16, 8), :] = cross[base:base + 16, 128 * t:128 * t + 128]
-
-    for j in order:
-        yy, zz = (y + j // 8) % NY, (z + j % 8) % NZ
-        block = pl.ds(pl.multiple_of((yy * NZ + zz) * 8, 8), 8)
-        send(S_OUT, dsnd.at[block, :], drcv.at[chip], dev(yy, zz, c, n))
-    drcv[chip] = dsnd[pl.ds(pl.multiple_of(chip * 8, 8), 8), :]
 
     got(S_BACK, brcv.at[pl.ds(0, 7)])
     slot_k = lax.broadcasted_iota(jnp.int32, (COMP, COMP), 1)
@@ -299,6 +291,26 @@
     for dn in (2, 1, 3):
         send(S_RES, esnd, ercv.at[n], dev(y, z, c, (n + dn) % NX))
     ercv[n] = esnd[...]
+
+    got(S_PLACED, placed_v.at[pl.ds(0, 3)])
+    cross = jnp.dot(placed_v[...].reshape(4 * SLICE, NC * DIES_DEV), mz_v[...], preferred_element_type=F32)
+    for nn in range(NX):
+        for kk in range(2):
+            for t in range(4):
+                base = 32 * nn + 16 * kk
+                dsnd[pl.ds(128 * nn + t * 2 + kk, 16, 8), :] = cross[base:base + 16, 128 * t:128 * t + 128]
+
+    for zz in range(NZ):
+        for dy in (0, 1, 7, 2, 6, 3, 5, 4):
+            yy = dy
+            block = pl.ds(pl.multiple_of((yy * NZ + zz) * 8, 8), 8)
+
+            @pl.when(chip != yy * NZ + zz)
+            def _(block=block, yy=yy, zz=zz):
+                send(S_OUT, dsnd.at[block, :], drcv.at[chip], dev(yy, zz, c, n))
+
+    drcv[chip] = dsnd[pl.ds(pl.multiple_of(chip * 8, 8), 8), :]
+
     got(S_RES, ercv.at[pl.ds(0, 3)])
     total = (ercv[0] + ercv[1]) + (ercv[2] + ercv[3])
     pick = jnp.where(n >= 2, total[1:2, :], total[0:1, :])
@@ -325,8 +337,17 @@
     sent(S_OUT, drcv.at[pl.ds(0, 63)])
 
 
+def finish(a_ref, b_ref, res_out, cross_out, sem):
+    one = pltpu.make_async_copy(a_ref, res_out, sem.at[0])
+    two = pltpu.make_async_copy(b_ref, cross_out, sem.at[1])
+    one.start()
+    two.start()
+    one.wait()
+    two.wait()
+
+
 def shards(iv_curves, mean_curve, loadings, metrology, dest_owner, dest_row):
-    any_spec = pl.BlockSpec(memory_space=pl.ANY)
+    hbm_spec = pl.BlockSpec(memory_space=pltpu.HBM)
     vmem_spec = pl.BlockSpec(memory_space=pltpu.VMEM)
     scratch = [
         pltpu.VMEM((DIES_DEV, FEAT), BF16),
@@ -337,8 +358,8 @@
         pltpu.VMEM((NC, DIES_DEV, METRO), BF16),
         pltpu.VMEM((NC * DIES_DEV, METRO), BF16),
         pltpu.VMEM((NC, 2, 2, 128), jnp.int32),
-        pltpu.VMEM((GROUP, SLICE, DIES_DEV), F32),
-        pltpu.VMEM((GROUP, SLICE, DIES_DEV), F32),
+        pltpu.VMEM((GROUP, SLICE, DIES_DEV), BF16),
+        pltpu.VMEM((GROUP, SLICE, DIES_DEV), BF16),
         pltpu.VMEM((NC, SLICE, DIES_DEV), BF16),
         pltpu.VMEM((GROUP, SLICE, DIES_DEV), BF16),
         pltpu.VMEM((1024, NC * DIES_DEV), BF16),
@@ -371,7 +392,7 @@
             jax.ShapeDtypeStruct((1, DIES_DEV // NX), F32),
             jax.ShapeDtypeStruct((2, METRO), F32),
         ),
-        in_specs=[any_spec] * 6,
+        in_specs=[hbm_spec] * 6,
         out_specs=(vmem_spec, vmem_spec),
         scratch_shapes=scratch,
         compiler_params=pltpu.CompilerParams(
@@ -385,6 +406,17 @@
         dest_owner.reshape(2, 128),
         dest_row.reshape(2, 128),
     )
+    any_spec = pl.BlockSpec(memory_space=pl.ANY)
+    residual, cross = pl.pallas_call(
+        finish,
+        out_shape=(
+            jax.ShapeDtypeStruct((1, DIES_DEV // NX), F32),
+            jax.ShapeDtypeStruct((2, METRO), F32),
+        ),
+        in_specs=[any_spec, any_spec],
+        out_specs=(any_spec, any_spec),
+        scratch_shapes=[pltpu.SemaphoreType.DMA((2,))],
+    )(residual, cross)
     return residual.reshape(DIES_DEV // NX), cross
 
 

time: 44 us -> 41.9 us (0.952)
  local copies, waits for them, and re-layouts: 1.74 us -> 0 us
    unnamed x6 -> x0, local copies, waits for them, and re-layouts: 1.74 us -> none
    pallas_call x1, Pallas kernels: 41.4 us -> 39.8 us  [shards(): pl.pallas_call(body, out_shape=(jax.ShapeDtypeStruct((1, DIES_DEV // NX),...]
    pallas_call x0 -> x1, Pallas kernels: none -> 1.26 us  [shards(): pl.pallas_call(finish, out_shape=(jax.ShapeDtypeStruct((1, DIES_DEV // NX...]
where the time goes in v3:
time: 41.9 us; the launch traced here: 41.7 us
  Pallas kernels  41.1 us (98%)
  between operations  0.64 us (2%)
    pallas_call x1, Pallas kernels, shards(): pl.pallas_call(body, out_shape=(jax.ShapeDtypeStruct((1, DIES_DEV // NX),...  39.8 us
    pallas_call x1, Pallas kernels, shards(): pl.pallas_call(finish, out_shape=(jax.ShapeDtypeStruct((1, DIES_DEV // NX...  1.26 us

profile of v3, /device:TPU:2, one launch (start us, length us, event | category | flops | bytes accessed | tf_op | source)
XLA Modules:
  0.0 41.7 jit_solution(16395813252198339197)
XLA Ops:
  0.6 39.8 %shard_map.77 = (f32[1,64]{1,0:T(1,128)}, f32[2,512]{1,0:T(2,128)}) custom-call(bf16[256,2048]{1,0:T(8,128)(2,1)} %iv_hbm.1, f32[1,2048]{1,0:T(1,128)} %bitcast.4, bf16[2048,256]{1,0:T(8,128)(2,1)} %load_hbm.1, bf16[256,512]{1,0:T(8,128)(2,1)} %met_hbm.1, s32[2,128]{1,0:T(2,128)} %bitcast.5, s32[2,128]{1,0:T(2,128)} %bitcast.6), custom_call_target="tpu_custom_call" | custom-call | flops 1000000000 | bytes 3000000 | tf_op jit(solution)/shard_map/pallas_call | solution.py:389
  40.4 1.3 %shard_map.78 = (f32[1,64]{1,0:T(1,128)}, f32[2,512]{1,0:T(2,128)}) custom-call(f32[1,64]{1,0:T(1,128)} %get-tuple-element.6.a_ref, f32[2,512]{1,0:T(2,128)} %get-tuple-element.7.b_ref), custom_call_target="tpu_custom_call" | custom-call | tf_op jit(solution)/shard_map/pallas_call | solution.py:410

commit v4 on v3

--- a/solution.py
+++ b/solution.py
@@ -75,10 +75,13 @@
     met_load = pltpu.make_async_copy(met_hbm, met_v.at[c], ld_sem.at[2 * CHUNKS + 1])
     own_load = pltpu.make_async_copy(own_hbm, route_v.at[c, 0], ld_sem.at[2 * CHUNKS + 2])
     row_load = pltpu.make_async_copy(row_hbm, route_v.at[c, 1], ld_sem.at[2 * CHUNKS + 3])
+    met_load.start()
     mean_load.start()
     for a, b in loads:
         a.start()
         b.start()
+    own_load.start()
+    row_load.start()
 
     barrier = pltpu.get_barrier_semaphore()
     for zz in z_peers:
@@ -88,9 +91,13 @@
     for cc, nn in group_peers:
         pl.semaphore_signal(barrier, inc=1, device_id=dev(y, z, cc, nn), device_id_type=MESH)
 
-    met_load.start()
-    own_load.start()
-    row_load.start()
+    met_load.wait()
+    met = met_v[c].astype(F32)
+    tot = jnp.sum(met, axis=0, keepdims=True)
+    sq = jnp.sum(met * met, axis=0, keepdims=True)
+    for t in range(4):
+        m1snd[t:t + 1, :] = tot[:, 128 * t:128 * t + 128]
+        m1snd[4 + t:5 + t, :] = sq[:, 128 * t:128 * t + 128]
 
     mean_load.wait()
     part = jnp.zeros((DIES_DEV, COMP), F32)
@@ -118,22 +125,14 @@
     for cc, nn in group_peers:
         q = cc * NX + nn
         send(S_SCORE, asnd.at[q], arcv.at[me8], dev(y, z, cc, nn))
+    for zz in z_peers:
+        send(S_M1, m1snd, m1rcv.at[z], dev(y, zz, c, n))
     for yy in y_peers:
         pl.semaphore_signal(plane_sem, inc=1, device_id=dev(yy, z, c, n), device_id_type=MESH)
 
-    met_load.wait()
-    met = met_v[c].astype(F32)
-    tot = jnp.sum(met, axis=0, keepdims=True)
-    sq = jnp.sum(met * met, axis=0, keepdims=True)
-    for t in range(4):
-        m1snd[t:t + 1, :] = tot[:, 128 * t:128 * t + 128]
-        m1snd[4 + t:5 + t, :] = sq[:, 128 * t:128 * t + 128]
     own_load.wait()
     row_load.wait()
-
     send(S_ROUTE, route_v.at[c], route_v.at[c], dev(y, z, 1 - c, n))
-    for zz in z_peers:
-        send(S_M1, m1snd, m1rcv.at[z], dev(y, zz, c, n))
     send(S_MET, met_v.at[c], met_v.at[c], dev(y, z, 1 - c, n))
     arcv[me8] = asnd[me8]
     m1rcv[z] = m1snd[...]
@@ -172,12 +171,6 @@
         oh_v[256 * l:256 * l + 256, :] = jnp.where(
             lax.broadcasted_iota(jnp.int32, (256, two), 0) + 256 * l == target, 1.0, 0.0).astype(BF16)
 
-    got(S_M1, m1rcv.at[pl.ds(0, 7)])
-    m2snd[...] = jnp.sum(m1rcv[...], axis=0)
-    for yy in y_peers:
-        send(S_M2, m2snd, m2rcv.at[y], dev(yy, z, c, n))
-    m2rcv[y] = m2snd[...]
-
     got(S_SCORE, arcv.at[pl.ds(0, 7)])
     halves = []
     for cs in range(NC):
@@ -201,6 +194,12 @@
     csnd[:, 4, :] = jnp.broadcast_to(stat, (CHIPS, 128))
 
     pl.semaphore_wait(plane_sem, len(y_peers))
+    got(S_M1, m1rcv.at[pl.ds(0, 7)])
+    m2snd[...] = jnp.sum(m1rcv[...], axis=0)
+    for yy in y_peers:
+        send(S_M2, m2snd, m2rcv.at[y], dev(yy, z, c, n))
+    m2rcv[y] = m2snd[...]
+
     order = sorted(range(1, CHIPS), key=lambda j: -(min(j // 8, 8 - j // 8) + min(j % 8, 8 - j % 8)))
     for j in order:
         yy, zz = (y + j // 8) % NY, (z + j % 8) % NZ
@@ -235,18 +234,6 @@
                 s16 = (2 * cp + cs) * 4 + l
                 ohr_v[cp, pl.ds(l * 128 + cs * 64, 64), :] = jnp.where(
                     rr[:, s16:s16 + 1] == spot, 1.0, 0.0).astype(BF16)
-
-    got(S_M3, m3rcv.at[0])
-    got(S_MET, met_v.at[0])
-    both = m3rcv[0] + m3rcv[1]
-    center = both[0:4, :] / TOTAL
-    scaling = lax.rsqrt(both[4:8, :] / TOTAL - center * center + EPSILON)
-    for cs in range(NC):
-        for t in range(4):
-            span = slice(128 * t, 128 * t + 128)
-            mz_v[256 * cs:256 * cs + 256, span] = (
-                (met_v[cs, :, span].astype(F32) - center[t:t + 1, :]) * scaling[t:t + 1, :]
-            ).astype(BF16)
 
     got(S_CHIP, crcv.at[pl.ds(0, 63)])
     stat = jnp.sum(crcv[:, 4, :], axis=0, keepdims=True)
@@ -268,6 +255,18 @@
 
     for dn in (2, 1, 3):
         send(S_PLACED, placed_v.at[n], placed_v.at[n], dev(y, z, c, (n + dn) % NX))
+
+    got(S_M3, m3rcv.at[0])
+    got(S_MET, met_v.at[0])
+    both = m3rcv[0] + m3rcv[1]
+    center = both[0:4, :] / TOTAL
+    scaling = lax.rsqrt(both[4:8, :] / TOTAL - center * center + EPSILON)
+    for cs in range(NC):
+        for t in range(4):
+            span = slice(128 * t, 128 * t + 128)
+            mz_v[256 * cs:256 * cs + 256, span] = (
+                (met_v[cs, :, span].astype(F32) - center[t:t + 1, :]) * scaling[t:t + 1, :]
+            ).astype(BF16)
 
     got(S_BACK, brcv.at[pl.ds(0, 7)])
     slot_k = lax.broadcasted_iota(jnp.int32, (COMP, COMP), 1)

time: 41.9 us -> 41.7 us (level)
  no operation moved by 1% of the time
where the time goes in v4:
time: 41.7 us; the launch traced here: 41.5 us
  Pallas kernels  40.9 us (98%)
  between operations  0.64 us (2%)
    pallas_call x1, Pallas kernels, shards(): pl.pallas_call(body, out_shape=(jax.ShapeDtypeStruct((1, DIES_DEV // NX),...  39.6 us
    pallas_call x1, Pallas kernels, shards(): pl.pallas_call(finish, out_shape=(jax.ShapeDtypeStruct((1, DIES_DEV // NX...  1.26 us

profile of v4, /device:TPU:2, one launch (start us, length us, event | category | flops | bytes accessed | tf_op | source)
XLA Modules:
  0.0 41.5 jit_solution(5771798826156470933)
XLA Ops:
  0.6 39.6 %shard_map.77 = (f32[1,64]{1,0:T(1,128)}, f32[2,512]{1,0:T(2,128)}) custom-call(bf16[256,2048]{1,0:T(8,128)(2,1)} %iv_hbm.1, f32[1,2048]{1,0:T(1,128)} %bitcast.4, bf16[2048,256]{1,0:T(8,128)(2,1)} %load_hbm.1, bf16[256,512]{1,0:T(8,128)(2,1)} %met_hbm.1, s32[2,128]{1,0:T(2,128)} %bitcast.5, s32[2,128]{1,0:T(2,128)} %bitcast.6), custom_call_target="tpu_custom_call" | custom-call | flops 1000000000 | bytes 3000000 | tf_op jit(solution)/shard_map/pallas_call | solution.py:388
  40.3 1.3 %shard_map.78 = (f32[1,64]{1,0:T(1,128)}, f32[2,512]{1,0:T(2,128)}) custom-call(f32[1,64]{1,0:T(1,128)} %get-tuple-element.6.a_ref, f32[2,512]{1,0:T(2,128)} %get-tuple-element.7.b_ref), custom_call_target="tpu_custom_call" | custom-call | tf_op jit(solution)/shard_map/pallas_call | solution.py:409
